TPU v7x, 32 devices: a whole 2x2x4 slice. The times are simulated.
32 devices in a mesh: seq: 16 (over z, y, core), row: 2 (over x).
Axes of the slice: x: 2, y: 2, z: 4, core: 2. Of those that a mesh axis runs over, the one named last changes fastest.
Arguments:
- layer_input: bfloat16 [2, 16384, 384], P('row', 'seq'), may hold values from -6 to 6
- segment_ids: int32 [2, 16384], P('row', 'seq'), may hold values from 0 to 63, never falling along the last dimension, each value on 1 to 512 neighbouring positions
- out_grad: bfloat16 [2, 16384, 384], P('row', 'seq'), may hold values from -6 to 6
- weights: float32 [1971840], P(('seq', 'row')), may hold values from -3 to 3
- momentum: float32 [1971840], P(('seq', 'row')), may hold values from -271.529 to 271.529
- average: float32 [1971840], P(('seq', 'row')), may hold values from -3 to 3
Outputs:
- block_output: bfloat16 [2, 16384, 384], P('row', 'seq')
- input_grad: float32 [2, 16384, 384], P('row', 'seq')
- weight_grad: float32 [1971840], P(('seq', 'row'))
- new_momentum: float32 [1971840], P(('seq', 'row'))
- new_average: float32 [1971840], P(('seq', 'row'))
- new_weights: float32 [1971840], P(('seq', 'row'))
- weight_copy: bfloat16 [1971840], P(('seq', 'row'))
Inputs may be any that keep to these rules, and one draw needn't show every extreme that they name: `segment_ids`: ids never fall along a row; every document holds 1 to 512 tokens and one of each row holds exactly 512.
All inputs are finite; a program needn't handle non-finite values.
Results may differ from a plain program's by a relative error of at most 0.012.
The roundings to bfloat16 on the way count: a program that leaves them out, or rounds other values in their place, can miss the bound.
Values may be sent and summed in bfloat16 or wider, within the bound.
A program may use at most 128 MiB of HBM per device.

v0:
```python
import functools
import itertools
import math

import jax
import jax.numpy as jnp
from jax import lax
from jax.experimental import pallas as pl
from jax.experimental.pallas import tpu as pltpu
from jax.sharding import PartitionSpec as P

D = 384
HEADS = 6
HEAD_DIM = 64
FF = 1536
SPAN = 256
PAIRS = HEADS // 2
NB = 5
EPSILON = 1e-07
(N_ATTN_GAIN, N_ATTN_SHIFT, N_CTX, N_DCTX_TURNED, N_DFLAT, N_DOWN_BIAS, N_DOWN_W, N_DVEC, N_DZ1, N_E, N_FFN_GAIN, N_FFN_SHIFT, N_INV, N_K, N_K_TURNED, N_K_TURNED_BACK, N_KEY_B, N_KEY_W, N_KRT, N_KRT_TURNED, N_OUT, N_OUTPUT_B, N_OUTPUT_W, N_POS, N_Q, N_Q_TURNED, N_QRT, N_QRT_TURNED, N_QUERY_B, N_QUERY_W, N_REL_GAIN, N_REL_SHIFT, N_REL_TABLE, N_SEG_EXT, N_UP_BIAS, N_UP_W, N_V, N_V_TURNED, N_VALUE_B, N_VALUE_W, N_VEC, N_X_EXT) = range(42)
bf = jnp.bfloat16
f32 = jnp.float32


MESH = pl.DeviceIdType.MESH
GROUP = 2048


class Grid:
    def __init__(self, seq, row):
        half = seq // 2
        wide = 1
        while wide * wide * 4 <= half:
            wide *= 2
        self.size = {"z": half // wide, "y": wide, "x": row}
        self.seq, self.row, self.count = seq, row, seq * row
        self.split = self.size["y"] == 2 and row == 2 and half > 4

    def here(self):
        s, x = lax.axis_index("seq"), lax.axis_index("row")
        y_size = self.size["y"]
        return {"z": s // (2 * y_size), "y": (s // 2) % y_size, "c": s % 2, "x": x}

    def seq_of(self, p):
        return (p["z"] * self.size["y"] + p["y"]) * 2 + p["c"]

    def flat(self, p):
        return self.seq_of(p) * self.row + p["x"]

    def device(self, p):
        return {"seq": self.seq_of(p), "row": p["x"]}

    def place(self, k):
        s, x = divmod(k, self.row)
        line, c = divmod(s, 2)
        z, y = divmod(line, self.size["y"])
        return z, y, c, x

    def plane(self, p):
        return (p["z"] * self.size["y"] + p["y"]) * self.row + p["x"]

    def offsets(self, order):
        choices = []
        for axis in order:
            n = self.size[axis]
            if n == 2:
                choices.append([0, "f"])
            else:
                choices.append([0] + [sign * d for d in range(1, n) for sign in (-1, 1)])
        hops = lambda off: sum(1 if o == "f" else abs(o) for o in off)
        return sorted(itertools.product(*choices), key=hops)


def both(conds):
    out = None
    for cond in conds:
        if cond is not None:
            out = cond if out is None else jnp.logical_and(out, cond)
    return out


def guarded(cond, fn):
    if cond is None:
        fn()
    else:
        pl.when(cond)(fn)


def source_of(grid, p, order, off):
    o, conds = dict(p), []
    for axis, d in zip(order, off):
        if d == "f":
            o[axis] = 1 - p[axis]
        elif d != 0:
            o[axis] = p[axis] + d
            conds.append(p[axis] + d >= 0 if d < 0 else p[axis] + d < grid.size[axis])
    return o, both(conds)


def parent_of(grid, p, order, off):
    last = max((i for i, d in enumerate(off) if d != 0), default=None)
    if last is None:
        return None, None
    q, axis, d = dict(p), order[last], off[last]
    if d == "f":
        q[axis] = 1 - p[axis]
        return q, axis + "0"
    q[axis] = p[axis] + (1 if d > 0 else -1)
    return q, axis + ("+" if d > 0 else "-")


def children_of(grid, p, order, off):
    last = max((i for i, d in enumerate(off) if d != 0), default=None)
    found = []
    if last is not None and off[last] != "f":
        axis, away = order[last], (-1 if off[last] > 0 else 1)
        q = dict(p)
        q[axis] = p[axis] + away
        found.append((axis + ("+" if away > 0 else "-"), q, p[axis] > 0 if away < 0 else p[axis] < grid.size[axis] - 1))
    for axis in order[0 if last is None else last + 1 :]:
        if grid.size[axis] == 2:
            q = dict(p)
            q[axis] = 1 - p[axis]
            found.append((axis + "0", q, None))
        elif grid.size[axis] > 2:
            for sign in (1, -1):
                q = dict(p)
                q[axis] = p[axis] + sign
                found.append((axis + ("+" if sign > 0 else "-"), q, p[axis] > 0 if sign < 0 else p[axis] < grid.size[axis] - 1))
    return found


def neighbours_of(grid, p):
    found = []
    for axis in ("z", "y", "x"):
        found += children_of(grid, p, (axis,), (0,))
    sibling = dict(p)
    sibling["c"] = 1 - p["c"]
    found.append(("c0", sibling, None))
    return found


def enter(grid, p, extra=()):
    sem = pltpu.get_barrier_semaphore()
    total = jnp.int32(0)
    for name, q, cond in neighbours_of(grid, p) + list(extra):
        guarded(cond, lambda q=q: pl.semaphore_signal(sem, inc=1, device_id=grid.device(q), device_id_type=MESH))
        total = total + (1 if cond is None else cond.astype(jnp.int32))
    pl.semaphore_wait(sem, total)


def parts_of(groups, whole):
    if whole:
        return ((("z", "y", "x"), 0, 16 * groups),)
    first = 16 * (groups // 2)
    return ((("z", "y", "x"), 0, first), (("x", "z", "y"), first, 16 * groups - first))


class Gather:
    def __init__(self, grid, p, slots, send_sem, recv_sem, groups):
        self.grid, self.p, self.slots = grid, p, slots
        self.send_sem, self.recv_sem, self.groups = send_sem, recv_sem, groups
        self.sends, self.used = [], 0

    def block(self, o, start, rows):
        return self.slots.at[o["z"], o["y"], o["c"], o["x"], pl.ds(start, rows), :]

    def copy(self, part, start, rows, o, q, index):
        block, k = self.block(o, start, rows), self.grid.flat(o)
        return pltpu.make_async_remote_copy(
            src_ref=block, dst_ref=block, send_sem=self.send_sem.at[index], recv_sem=self.recv_sem.at[part, k],
            device_id=self.grid.device(q), device_id_type=MESH)

    def arrived(self, part, start, rows, o):
        block, k = self.block(o, start, rows), self.grid.flat(o)
        pltpu.make_async_remote_copy(
            src_ref=block, dst_ref=block, send_sem=self.send_sem.at[0], recv_sem=self.recv_sem.at[part, k],
            device_id=self.grid.device(self.p), device_id_type=MESH).wait_recv()

    def plan(self, chosen, whole, used):
        grid, p = self.grid, self.p
        sibling = dict(p)
        sibling["c"] = 1 - p["c"]
        levels, ends, partners = {}, [], []
        for part, (order, start, rows) in enumerate(parts_of(self.groups, whole)):
            for off in grid.offsets(order):
                hops = sum(1 if o == "f" else abs(o) for o in off)
                o, cond = source_of(grid, p, order, off)
                k = grid.flat(o)
                targets = children_of(grid, p, order, off) + [("c0", sibling, None)]
                indices = [used + i for i in range(len(targets))]
                used += len(targets)
                cond = both([cond, chosen(o)])

                def step(what=(part, start, rows, o), targets=targets, indices=indices, own=hops == 0):
                    if not own:
                        self.arrived(*what)
                    for (name, q, when), index in zip(targets, indices):
                        guarded(when, lambda q=q, index=index: self.copy(*what, q, index).start())

                def end(what=(part, start, rows, o), targets=targets, indices=indices):
                    for (name, q, when), index in zip(targets, indices):
                        guarded(when, lambda q=q, index=index: self.copy(*what, q, index).wait_send())

                levels.setdefault(hops, []).append((cond, step))
                ends.append((cond, end))
                o, cond = source_of(grid, sibling, order, off)
                k = grid.flat(o)
                partners.append((both([cond, chosen(o)]), lambda what=(part, start, rows, o): self.arrived(*what)))
        return [levels[h] for h in sorted(levels)], partners, ends


def perform(steps):
    for cond, step in steps:
        guarded(cond, step)


def count_sends(grid, groups, whole):
    fake = {"z": jnp.int32(0), "y": jnp.int32(0), "x": jnp.int32(0), "c": jnp.int32(0)}
    return sum(len(children_of(grid, fake, order, off)) + 1 for order, _, _ in parts_of(groups, whole) for off in grid.offsets(order))


OPPOSITE = {"+": "-", "-": "+", "0": "0"}


def direction_names(grid):
    names = ["c0"]
    for axis in ("z", "y", "x"):
        if grid.size[axis] == 2:
            names.append(axis + "0")
        elif grid.size[axis] > 2:
            names += [axis + "+", axis + "-"]
    return names


class Scatter:
    def __init__(self, grid, p, flat, first_row, kids, total, send_sem, recv_sem, groups):
        self.grid, self.p, self.flat, self.first_row = grid, p, flat, first_row
        self.kids, self.total = kids, total
        self.send_sem, self.recv_sem, self.groups = send_sem, recv_sem, groups
        self.names = direction_names(grid)

    def incoming(self, part, name, place):
        start, rows = self.spans[part]
        return self.kids.at[self.names.index(name), place, pl.ds(start, rows), :]

    def transfer(self, source, part, name, place, q, send):
        return pltpu.make_async_remote_copy(
            src_ref=source, dst_ref=self.incoming(part, name, place), send_sem=self.send_sem.at[send],
            recv_sem=self.recv_sem.at[part, self.names.index(name), place], device_id=self.grid.device(q), device_id_type=MESH)

    def arrived(self, part, name, place):
        block = self.incoming(part, name, place)
        pltpu.make_async_remote_copy(
            src_ref=block, dst_ref=block, send_sem=self.send_sem.at[0],
            recv_sem=self.recv_sem.at[part, self.names.index(name), place],
            device_id=self.grid.device(self.p), device_id_type=MESH).wait_recv()

    def plan(self, result, chosen, whole, used):
        grid, p = self.grid, self.p
        sibling = dict(p)
        sibling["c"] = 1 - p["c"]
        gifts, levels, ends = [], {}, []
        self.spans = [part[1:] for part in parts_of(self.groups, whole)]
        for part, (order, start, rows) in enumerate(parts_of(self.groups, whole)):
            for off in sorted(grid.offsets(order), key=lambda off: -sum(1 if o == "f" else abs(o) for o in off)):
                hops = sum(1 if o == "f" else abs(o) for o in off)
                o, cond = source_of(grid, sibling, order, off)
                cond = both([cond, chosen(grid.flat(o))])

                def give(part=part, o=o, index=used, start=start, rows=rows):
                    block = self.flat.at[pl.ds(pl.multiple_of(self.first_row(grid.flat(o)) + start, 16), rows), :]
                    return self.transfer(block, part, "c0", grid.plane(o), sibling, index)

                gifts.append((cond, lambda give=give: give().start()))
                ends.append((cond, lambda give=give: give().wait_send()))
                used += 1
                o, cond = source_of(grid, p, order, off)
                place, k = grid.plane(o), grid.flat(o)
                cond = both([cond, chosen(k)])
                kids = children_of(grid, p, order, off)
                parent, side = parent_of(grid, p, order, off)

                def push(part=part, place=place, parent=parent, side=side, index=used, start=start, rows=rows):
                    return self.transfer(self.incoming(part, "c0", place), part, side[0] + OPPOSITE[side[1]], place, parent, index)

                def step(part=part, place=place, k=k, kids=kids, parent=parent, start=start, rows=rows, push=push):
                    self.arrived(part, "c0", place)
                    mine = self.flat[pl.ds(pl.multiple_of(self.first_row(k) + start, 16), rows), :].astype(f32)
                    self.total[0:rows, :] = mine + self.incoming(part, "c0", place)[...].astype(f32)
                    for name, q, when in kids:

                        def add(name=name):
                            self.arrived(part, name, place)
                            self.total[0:rows, :] += self.incoming(part, name, place)[...].astype(f32)

                        guarded(when, add)
                    if parent is None:
                        result[pl.ds(start, rows), :] = self.total[0:rows, :]
                    else:
                        self.kids[0, place, pl.ds(start, rows), :] = self.total[0:rows, :].astype(bf)
                        push().start()

                levels.setdefault(-hops, []).append((cond, step))
                if parent is not None:
                    ends.append((cond, lambda push=push: push().wait_send()))
                    used += 1
        return gifts, [levels[h] for h in sorted(levels)], ends


def scatter_sends(grid, groups, whole):
    return 2 * sum(len(grid.offsets(order)) for order, _, _ in parts_of(groups, whole))


def shard_groups(shard, count):
    first = [shard * k // GROUP for k in range(count)]
    groups = max(-(-shard * (k + 1) // GROUP) - first[k] for k in range(count))
    return first, max(groups, 2)


def flat_rows(shard, count):
    first, groups = shard_groups(shard, count)
    return 16 * (first[-1] + groups)


def layer_pieces():
    square, vector_of = (D, D), (D,)
    return (
        (N_QUERY_W, square), (N_KEY_W, square), (N_VALUE_W, square), (N_OUTPUT_W, square), (N_UP_W, (D, FF)), (N_DOWN_W, (FF, D)),
        (N_QUERY_B, vector_of), (N_KEY_B, vector_of), (N_VALUE_B, vector_of), (N_OUTPUT_B, vector_of), (N_ATTN_GAIN, vector_of),
        (N_ATTN_SHIFT, vector_of), (N_UP_BIAS, (FF,)), (N_DOWN_BIAS, vector_of), (N_FFN_GAIN, vector_of), (N_FFN_SHIFT, vector_of),
        (N_REL_TABLE, (2 * SPAN, D)), (N_REL_GAIN, vector_of), (N_REL_SHIFT, vector_of),
    )


def matrix_rows():
    place, at = {}, 0
    for name, extent in layer_pieces():
        if len(extent) == 2:
            place[name] = (at // 128, extent[0], extent[1] // 128)
        else:
            place[name] = (at // 128, 1, extent[0] // 128)
        at += math.prod(extent)
    return place


MATRICES = (N_QUERY_W, N_KEY_W, N_VALUE_W, N_OUTPUT_W, N_UP_W, N_DOWN_W, N_REL_TABLE)
VECTORS = tuple(name for name, extent in layer_pieces() if len(extent) == 1)
FEED_FIRST = matrix_rows()[N_OUTPUT_W][0]
FEED_ROWS = matrix_rows()[N_QUERY_B][0] - FEED_FIRST
USED_ROWS = sum(rows * pieces for _, rows, pieces in matrix_rows().values())


def vector_rows():
    place, at = {}, 0
    for name in VECTORS:
        wide = matrix_rows()[name][2]
        place[name] = (at, wide)
        at += wide
    return place, -(-at // 8) * 8


SC = 1.0 / math.sqrt(3.0 * HEAD_DIM)
LOG2E = 1.4426950408889634
NT = (((1,), (1,)), ((), ()))
NN = (((1,), (0,)), ((), ()))
TN = (((0,), (0,)), ((), ()))


def dot(a, b, dims=NN):
    return lax.dot_general(a, b, dims, preferred_element_type=f32)


def iotas(rows, lanes):
    return lax.broadcasted_iota(jnp.int32, (rows, lanes), 0), lax.broadcasted_iota(jnp.int32, (rows, lanes), 1)


def tile(i):
    return pl.ds(pl.multiple_of(i * 128, 128), 128)


def window(i):
    return pl.ds(pl.multiple_of(i * 128, 128), NB * 128)


def wide_diagonal(columns):
    zero = jnp.zeros((64, 128), columns.dtype)
    return jnp.concatenate([jnp.concatenate([columns[:64], zero], axis=1), jnp.concatenate([zero, columns[64:]], axis=1)], axis=0)


def tall_diagonal(rows):
    lane = iotas(128, 128)[1]
    zero = jnp.zeros_like(rows)
    return jnp.concatenate([jnp.where(lane < 64, rows, zero), jnp.where(lane >= 64, rows, zero)], axis=0)


def own_heads(wide):
    return jnp.concatenate([wide[:64, :128], wide[64:, 128:]], axis=0)


def turn_rows(values, back):
    size = values.shape[0]
    lane = iotas(*values.shape)[1]
    for step in (64, 32, 16, 8, 4, 2, 1):
        moved = pltpu.roll(values, size - step if back else step, 0)
        values = jnp.where(lane & step != 0, moved, values)
    return values


def turn_lanes(values, first):
    return jnp.concatenate([pltpu.roll(values[8 * g : 8 * g + 8, :512], first + 8 * g, 1, stride=1, stride_axis=0) for g in range(16)], axis=0)


def stream_rows(load, up, fine):
    row, lane = iotas(8, 128)
    inner = [(step, lane & step != 0, row < step if not up else row >= 8 - step) for step in fine]
    masks = [lane & step != 0 for step in (8, 16, 32, 64)]
    turned = [None for _ in inner]
    past = [[] for _ in masks]
    extra = 15 + len(inner)
    order = list(range(64 - extra, 64)) + list(range(64)) if not up else list(reversed(list(range(64)) + list(range(extra))))
    for n, i in enumerate(order):
        value = load(i)
        for level, (step, mask, edge) in enumerate(inner):
            now = pltpu.roll(value, step if not up else 8 - step, 0)
            if turned[level] is not None:
                value = jnp.where(mask, jnp.where(edge, turned[level], now), value)
            turned[level] = now
        for level, mask in enumerate(masks):
            past[level].append(value)
            if len(past[level]) > 1 << level:
                value = jnp.where(mask, past[level].pop(0), value)
        if n >= extra:
            yield i, value


def att_fwd_body(nblk, qT_ref, k_ref, vT_ref, krt_ref, qrtT_ref, seg_ref, ctx_ref, p_ref, inv_ref, x_scr, bias_scr, s0, s1, z0, z1, t0, t1, m0, m1, hook=None):
    row, lane = iotas(128, 128)
    lane2 = iotas(128, 256)[1]
    lane512 = iotas(512, 256)[1]
    items, keys = PAIRS * nblk, nblk + 4

    def mk_bias(t, carry):
        sq = seg_ref[0:1, tile(t + 2)].astype(f32)
        for b in range(NB):
            sk = jnp.broadcast_to(seg_ref[0:1, tile(t + b)], (128, 128)).astype(f32).T
            ok = sk == sq
            if b == 0:
                ok = ok & (row >= lane)
            if b == NB - 1:
                ok = ok & (row <= lane)
            bias_scr[t, 128 * b : 128 * b + 128, :] = jnp.where(ok, 0.0, -1e30).astype(f32)
        return carry

    lax.fori_loop(0, nblk, mk_bias, 0)

    def keyside(p, J, slot):
        C = dot(tall_diagonal(k_ref[p, tile(J), :]), qrtT_ref[p])
        for h in range(2):
            Ch = C[128 * h : 128 * h + 128]
            R = turn_lanes(Ch, 0)
            x_scr[slot, h, :, 0:128] = jnp.where(lane > row, R[:, :128], Ch[:, 512:]).astype(bf)
            x_scr[slot, h, :, 128:512] = R[:, 128:].astype(bf)
            x_scr[slot, h, :, 512:640] = R[:, :128].astype(bf)

    def start(J, carry):
        keyside(0, J, J)
        return carry

    lax.fori_loop(0, keys, start, 0)

    def scores(n, s_scr, z_scr, t_scr, m_scr):
        n = jnp.minimum(n, items - 1)
        p, t = n // nblk, n % nblk
        base = (p % 2) * keys + t
        Q2 = wide_diagonal(qT_ref[p, :, tile(t)])
        odd = lane2 % 2 == 1
        zero = jnp.zeros_like(Q2)
        table = krt_ref[p]
        moved = krt_ref[PAIRS + p]
        Z = dot(jnp.concatenate([table, moved], axis=1), jnp.concatenate([jnp.where(odd, zero, Q2), jnp.where(odd, Q2, zero)], axis=0))
        ends = jnp.where(odd[:1], Z[2:3], Z[1:2])
        z_scr[...] = Z
        s_scr[...] = dot(k_ref[p, window(t), :], Q2)
        for h in range(2):
            cols = slice(128 * h, 128 * h + 128)

            def load(i):
                return z_scr[8 * i : 8 * i + 8, cols]

            end = ends[:, cols]
            top = None
            held = None
            for i, y in stream_rows(load, False, (2, 4)):
                if i % 2 == 0:
                    held = y
                    continue
                at, b = 8 * (i - 1), i // 16
                y = jnp.concatenate([held, y], axis=0)
                for block in (0, 4) if b == 0 else (b,):
                    r = at + 128 * (block - b)
                    rows = slice(r, r + 16)
                    inner = slice(at % 128, at % 128 + 16)
                    x = x_scr[base + block, h, inner, 128 * (4 - block) : 128 * (5 - block)].astype(f32)
                    part = y
                    if block == 0:
                        part = jnp.where(iotas(16, 128)[0] + at > iotas(16, 128)[1], y, end)
                    T = s_scr[rows, cols] + bias_scr[t, rows, :] + part + x
                    t_scr[rows, cols] = T
                    most = jnp.maximum(T[:8], T[8:])
                    top = most if top is None else jnp.maximum(top, most)
            m_scr[:, cols] = top

    def soft(n, t_scr, m_scr):
        n = jnp.clip(n, 0, items - 1)
        m = jnp.max(m_scr[...], axis=0, keepdims=True)
        total = None
        for i in range(40):
            e = jnp.exp2((t_scr[16 * i : 16 * i + 16, :] - m) * (SC * LOG2E))
            part = e[:8] + e[8:]
            total = part if total is None else total + part
            p_ref[n // nblk, n % nblk, 16 * i : 16 * i + 16, :] = e.astype(bf)
        inv_ref[n // nblk, n % nblk] = jnp.broadcast_to(1.0 / jnp.sum(total, axis=0, keepdims=True), (8, 256))

    def context(n):
        n = jnp.clip(n, 0, items - 1)
        p, t = n // nblk, n % nblk
        ctxT = own_heads(dot(vT_ref[p, :, window(t)], p_ref[p, t]) * inv_ref[p, t, 0:1, :])
        ctx_ref[p, tile(t), :] = ctxT.astype(bf).T

    half = nblk // 2
    per = keys // half

    def body(m, slot):
        context(2 * m - 2)
        soft(2 * m - 1, t1, m1)
        scores(2 * m, s0, z0, t0, m0)
        context(2 * m - 1)
        soft(2 * m, t0, m0)
        scores(2 * m + 1, s1, z1, t1, m1)
        p, first = jnp.minimum(m // half + 1, PAIRS - 1), per * (m % half)
        for i in range(per):
            keyside(p, first + i, slot + i)
        if hook is not None:
            hook(m)
        return jnp.where(slot + per == 2 * keys, 0, slot + per)

    lax.fori_loop(0, items // 2 + 1, body, jnp.int32(keys))


def unreversed(values, JR):
    high = values.astype(bf)
    low = (values - high.astype(f32)).astype(bf)
    both = dot(JR, jnp.concatenate([high, low], axis=1))
    return both[:, :128] + both[:, 128:]


def att_bwd_body(nblk, q_ref, kT_ref, kTr_ref, v_ref, krtT_ref, qrt_ref, qrtT_ref, dctxT_ref, e_ref, inv_ref, dq_ref, dkc_ref, dkp_ref, dv_ref, dkr_ref, dqr_ref,
                 gt_scr, dp_scr, gm_scr, gb0, gb1, gu0, gu1, e_scr, e_sem, hook):
    row, lane = iotas(128, 128)
    row16, lane16 = iotas(16, 256)
    JR = (row + lane == 127).astype(bf)
    zero = jnp.zeros((128, 128), bf)
    items, keys, half = PAIRS * nblk, nblk + 4, nblk // 2
    per = keys // half
    gt_scr[...] = jnp.zeros(gt_scr.shape, bf)
    gb1[...] = jnp.zeros(gb1.shape, bf)
    gu1[...] = jnp.zeros(gu1.shape, bf)
    for ref in (dkc_ref, dv_ref, dkr_ref, dqr_ref):
        ref[...] = jnp.zeros(ref.shape, f32)

    def kblocks(p, first, base):
        turned = [[], []]
        for i in range(per):
            for h in range(2):
                GT = gt_scr[base + first + i, h]
                Gm = jnp.concatenate([jnp.where(lane > row, GT[:, :128], GT[:, 512:]), GT[:, 128:512]], axis=1)
                turned[h].append(turn_lanes(dot(JR, Gm), 385).astype(bf))
        stacked = [jnp.concatenate(part, axis=0) for part in turned]
        dk = dot(jnp.concatenate(stacked, axis=1), qrt_ref[p])
        for i in range(per):
            dkp_ref[p, tile(first + i), :] = unreversed(dk[128 * i : 128 * i + 128], JR)
        span = pl.ds(pl.multiple_of(first * 128, 128), 128 * per)
        for h in range(2):
            heads = slice(64 * h, 64 * h + 64)
            dqr_ref[p, heads, 0:512] += dot(kTr_ref[p, heads, span], stacked[h])

    def upstream(n, slot, gb, gu, held):
        p, t = n // nblk, n % nblk
        D2 = wide_diagonal(dctxT_ref[p, :, tile(t)])
        inv = inv_ref[p, t, 0:1, :]
        dp_scr[...] = dot(v_ref[p, window(t), :], D2)
        total = None
        for i in range(40):
            rows = slice(16 * i, 16 * i + 16)
            w = e_scr[held, rows, :].astype(f32) * dp_scr[rows, :]
            part = w[:8] + w[8:]
            total = part if total is None else total + part
        less = jnp.sum(total, axis=0, keepdims=True) * inv * inv

        def grad(i):
            rows = slice(16 * i, 16 * i + 16)
            G = e_scr[held, rows, :].astype(f32) * (dp_scr[rows, :] * inv - less)
            Gb = G.astype(bf)
            gb[rows, :] = Gb
            b = i // 8
            for h in range(2):
                gt_scr[slot + b, h, 16 * (i % 8) : 16 * (i % 8) + 16, 128 * (4 - b) : 128 * (5 - b)] = Gb[:, 128 * h : 128 * h + 128]
            return G

        ends = None
        final = None
        for i in range(32):
            G = grad(i)
            if i < 8:
                at = row16 + 16 * i - lane16 % 128
                part = jnp.where(at == 0, G, 0.0)
                part = part[:8] + part[8:]
                ends = part if ends is None else ends + part
                other = grad(32 + i)
                part = jnp.where(at == 0, other, 0.0)
                part = part[:8] + part[8:]
                final = part if final is None else final + part
                G = jnp.where(at > 0, G, other)
            gm_scr[16 * i : 16 * i + 16, :] = G
        ends = jnp.sum(ends, axis=0, keepdims=True)
        final = jnp.sum(final, axis=0, keepdims=True)
        final = jnp.concatenate([jnp.broadcast_to(final[:, :128], (64, 128)), jnp.broadcast_to(final[:, 128:], (64, 128))], axis=0)
        dqr_ref[p, :, 512:640] += kT_ref[p, :, tile(t + 4)].astype(f32) * final
        dkc_ref[p, tile(t + 4), :] += (qrtT_ref[p, :, 512:640].astype(f32) * final).T
        dv_ref[p, window(t), :] += dot(e_scr[held], (D2.astype(f32) * inv).astype(bf).T)
        for h in range(2):
            cols = slice(128 * h, 128 * h + 128)
            held = None
            for i, y in stream_rows(lambda i: gm_scr[8 * i : 8 * i + 8, cols], True, (1, 2, 4)):
                if i == 0:
                    y = y + jnp.where(row[:8] == 1, ends[:, cols], 0.0)
                if i % 2 == 1:
                    held = y
                else:
                    gu[8 * i : 8 * i + 16, cols] = jnp.concatenate([y, held], axis=0).astype(bf)

    def downstream(n, gb, gu):
        n = jnp.maximum(n, 0)
        p, t = n // nblk, n % nblk
        dqT = own_heads(dot(kT_ref[p, :, window(t)], gb[...]) + dot(krtT_ref[p], gu[...]))
        dq_ref[p, tile(t), :] = (SC * dqT).astype(bf).T
        Qm = tall_diagonal(q_ref[p, tile(t), :])
        dkc_ref[p, window(t), :] += dot(gb[...], Qm)
        dkr_ref[p] += dot(gu[...], Qm)

    def fetch(m):
        source = e_ref.at[m // half, pl.ds(2 * (m % half), 2)]
        return pltpu.make_async_copy(source, e_scr.at[pl.ds(2 * (m % 2), 2)], e_sem.at[m % 2])

    def body(m, slot, late):
        p = m // half
        fetch(m).wait()
        pl.when(m + 1 < items // 2)(lambda: fetch(m + 1).start())
        if late:
            kblocks(p - 1, per * (m % half), (1 - p % 2) * keys)
        downstream(2 * m - 1, gb1, gu1)
        upstream(2 * m, slot, gb0, gu0, 2 * (m % 2))
        downstream(2 * m, gb0, gu0)
        upstream(2 * m + 1, slot + 1, gb1, gu1, 2 * (m % 2) + 1)
        hook(m)
        following = slot + 2
        following = jnp.where(following == nblk, keys, following)
        return jnp.where(following == keys + nblk, 0, following)

    fetch(jnp.int32(0)).start()
    slot = lax.fori_loop(0, half, lambda m, slot: body(m, slot, False), jnp.int32(0))
    lax.fori_loop(half, items // 2, lambda m, slot: body(m, slot, True), slot)
    downstream(items - 1, gb1, gu1)

    def last(i, carry):
        kblocks(PAIRS - 1, per * i, ((PAIRS - 1) % 2) * keys)
        return carry

    lax.fori_loop(0, half, last, 0)


def vector(vec_ref, name):
    at, wide = vector_rows()[0][name]
    return jnp.concatenate([vec_ref[at + i : at + i + 1, :] for i in range(wide)], axis=1)


def put_vector(vec_ref, name, value):
    at, wide = vector_rows()[0][name]
    for i in range(wide):
        vec_ref[at + i : at + i + 1, :] = value[:, 128 * i : 128 * i + 128]


def add_vector(vec_ref, name, value):
    at, wide = vector_rows()[0][name]
    for i in range(wide):
        vec_ref[at + i : at + i + 1, :] += value[:, 128 * i : 128 * i + 128]


def normalized(values):
    centered = values - jnp.mean(values, axis=1, keepdims=True)
    inverse = lax.rsqrt(jnp.mean(centered * centered, axis=1, keepdims=True) + EPSILON)
    return centered * inverse, inverse


def norm_back(upstream, gain, unit, inverse):
    scaled = upstream * gain
    mean = jnp.mean(scaled, axis=1, keepdims=True)
    along = jnp.mean(scaled * unit, axis=1, keepdims=True)
    return inverse * (scaled - mean - unit * along)


def column_sum(values):
    return jnp.sum(values, axis=0, keepdims=True)


def reversal():
    row = lax.broadcasted_iota(jnp.int32, (128, 128), 0)
    lane = lax.broadcasted_iota(jnp.int32, (128, 128), 1)
    return (row + lane == 127).astype(bf)


def reversed_rows(values, JR):
    blocks = values.shape[0] // 128
    return jnp.concatenate([dot(JR, values[128 * b : 128 * b + 128]).astype(bf) for b in reversed(range(blocks))], axis=0)


def project_body(x_ref, query_w, key_w, value_w, table_ref, vec_ref, q_ref, qT_ref, k_ref, kT_ref, kTr_ref, v_ref, vT_ref, krt_ref, krtT_ref, qrt_ref, qrtT_ref, pos_ref):
    tokens = q_ref.shape[1]
    JR = reversal()
    lane = iotas(512, 128)[1]
    unit, _ = normalized(table_ref[...].astype(f32))
    pos = (unit * vector(vec_ref, N_REL_GAIN) + vector(vec_ref, N_REL_SHIFT)).astype(bf)
    pos = pltpu.roll(reversed_rows(pos, JR).astype(f32), 1, 0).astype(bf)
    pos_ref[...] = pos
    keys = dot(pos, key_w[...]) + vector(vec_ref, N_KEY_B)
    moved = pltpu.roll(keys, 1, 0).astype(bf)
    keys = keys.astype(bf)
    queries = (dot(pos, query_w[...]) + vector(vec_ref, N_QUERY_B)).astype(bf)
    for p in range(PAIRS):
        cols = slice(128 * p, 128 * p + 128)
        krt_ref[p] = keys[:, cols]
        krt_ref[PAIRS + p] = moved[:, cols]
        krtT_ref[p] = keys[:, cols].T
        qrtT_ref[p, :, 0:512] = queries[:, cols].T
        qrtT_ref[p, :, 512:640] = jnp.broadcast_to(queries[1:2, cols], (128, 128)).T
        zero = jnp.zeros((512, 128), bf)
        qrt_ref[p, 0:512, :] = jnp.where(lane < 64, queries[:, cols], zero)
        qrt_ref[p, 512:1024, :] = jnp.where(lane < 64, zero, queries[:, cols])
    bias = {name: vector(vec_ref, name) for name in (N_QUERY_B, N_KEY_B, N_VALUE_B)}

    def chunk(i, carry):
        rows = pl.ds(pl.multiple_of(i * 256, 256), 256)
        x = x_ref[rows, :]
        y = (dot(x, key_w[...]) + bias[N_KEY_B]).astype(bf)
        w = (dot(x, value_w[...]) + bias[N_VALUE_B]).astype(bf)
        for p in range(PAIRS):
            cols = slice(128 * p, 128 * p + 128)
            k_ref[p, rows, :] = y[:, cols]
            turned = y[:, cols].T
            kT_ref[p, :, rows] = turned
            kTr_ref[p, :, rows] = jnp.concatenate([dot(turned[:, :128], JR), dot(turned[:, 128:], JR)], axis=1).astype(bf)
            v_ref[p, rows, :] = w[:, cols]
            vT_ref[p, :, rows] = w[:, cols].T
        return carry

    lax.fori_loop(0, x_ref.shape[0] // 256, chunk, 0)

    def own(i, carry):
        rows = pl.ds(pl.multiple_of(i * 256, 256), 256)
        x = x_ref[pl.ds(pl.multiple_of(i * 256 + SPAN, 256), 256), :]
        y = (dot(x, query_w[...]) + bias[N_QUERY_B]).astype(bf)
        for p in range(PAIRS):
            q_ref[p, rows, :] = y[:, 128 * p : 128 * p + 128]
            qT_ref[p, :, rows] = y[:, 128 * p : 128 * p + 128].T
        return carry

    lax.fori_loop(0, tokens // 256, own, 0)


SQRT_HALF = 0.7071067811865476
PHI_SCALE = 0.3989422804014327


def gelu_and_slope(u):
    cdf = 0.5 + 0.5 * lax.erf(u * SQRT_HALF)
    return u * cdf, cdf + u * (PHI_SCALE * jnp.exp(-0.5 * u * u))


def feed_body(x_ref, ctx_ref, og_ref, output_w, up_w, down_w, vec_ref, out_ref, dz1_ref, dctx_ref, wide, dvec_ref,
              ml_scr, dup_scr, act_scr, ddown_scr, dattn_scr, slope_scr):
    tokens = out_ref.shape[0]
    dvec_ref[...] = jnp.zeros(dvec_ref.shape, f32)
    vecs = {name: vector(vec_ref, name) for name in (N_OUTPUT_B, N_ATTN_GAIN, N_ATTN_SHIFT, N_UP_BIAS, N_DOWN_BIAS, N_FFN_GAIN, N_FFN_SHIFT)}
    C = 256

    def chunk(i, carry):
        rows = pl.ds(pl.multiple_of(i * C, C), C)
        h = x_ref[pl.ds(pl.multiple_of(i * C + SPAN, C), C), :].astype(f32)
        z1 = h + dot(jnp.concatenate([ctx_ref[p, rows, :] for p in range(PAIRS)], axis=1), output_w[...]) + vecs[N_OUTPUT_B]
        unit1, inv1 = normalized(z1)
        mid = unit1 * vecs[N_ATTN_GAIN] + vecs[N_ATTN_SHIFT]
        ml = mid.astype(bf)
        ml_scr[rows, :] = ml
        z2 = mid + vecs[N_DOWN_BIAS]
        for f in range(FF // 256):
            cols = slice(256 * f, 256 * f + 256)
            up = dot(ml, up_w[:, cols]) + vecs[N_UP_BIAS][:, cols]
            act, slope = gelu_and_slope(up)
            act_scr[rows, cols] = act.astype(bf)
            slope_scr[:, cols] = slope
        z2 = z2 + dot(act_scr[rows, :], down_w[...])
        unit2, inv2 = normalized(z2)
        out_ref[rows, :] = (unit2 * vecs[N_FFN_GAIN] + vecs[N_FFN_SHIFT]).astype(bf)
        dh = og_ref[rows, :].astype(f32)
        add_vector(dvec_ref, N_FFN_GAIN, column_sum(dh * unit2))
        add_vector(dvec_ref, N_FFN_SHIFT, column_sum(dh))
        dz2 = norm_back(dh, vecs[N_FFN_GAIN], unit2, inv2)
        ddown = dz2.astype(bf)
        ddown_scr[rows, :] = ddown
        add_vector(dvec_ref, N_DOWN_BIAS, column_sum(ddown.astype(f32)))
        for f in range(FF // 256):
            cols = slice(256 * f, 256 * f + 256)
            dup = (dot(ddown, down_w[cols, :], NT) * slope_scr[:, cols]).astype(bf)
            dup_scr[rows, cols] = dup
        add_vector(dvec_ref, N_UP_BIAS, column_sum(dup_scr[rows, :].astype(f32)))
        dmid = dz2 + dot(dup_scr[rows, :], up_w[...], NT)
        add_vector(dvec_ref, N_ATTN_GAIN, column_sum(dmid * unit1))
        add_vector(dvec_ref, N_ATTN_SHIFT, column_sum(dmid))
        dz1 = norm_back(dmid, vecs[N_ATTN_GAIN], unit1, inv1)
        dz1_ref[rows, :] = dz1
        dattn = dz1.astype(bf)
        dattn_scr[rows, :] = dattn
        add_vector(dvec_ref, N_OUTPUT_B, column_sum(dattn.astype(f32)))
        dctx = dot(dattn, output_w[...], NT).astype(bf)
        for p in range(PAIRS):
            dctx_ref[p, :, rows] = dctx[:, 128 * p : 128 * p + 128].T
        return carry

    lax.fori_loop(0, tokens // C, chunk, 0)
    place = matrix_rows()

    def put(name, first, rows, value):
        base, _, pieces = place[name]
        for c in range(value.shape[1] // 128):
            wide[pl.ds(base - FEED_FIRST + pieces * first[0] + first[1] + c, rows, stride=pieces), :] = value[:, 128 * c : 128 * c + 128]

    ctx = jnp.concatenate([ctx_ref[p] for p in range(PAIRS)], axis=1)
    put(N_OUTPUT_W, (0, 0), D, dot(ctx, dattn_scr[...], TN))
    for f in range(FF // 256):
        cols = slice(256 * f, 256 * f + 256)
        put(N_UP_W, (0, 2 * f), D, dot(ml_scr[...], dup_scr[:, cols], TN))
        put(N_DOWN_W, (256 * f, 0), 256, dot(act_scr[:, cols], ddown_scr[...], TN))


def split(values):
    high = values.astype(bf)
    return high, (values - high.astype(f32)).astype(bf)


def dot2(left, right, dims=NN):
    if left.dtype == f32:
        return sum(dot(part, right, dims) for part in split(left))
    return sum(dot(left, part, dims) for part in split(right))


def tail_local(dq_ref, x_ref, query_w, dx_ref, dwq_ref, dvec_ref):
    tokens = dx_ref.shape[0]
    dq = jnp.concatenate([dq_ref[p] for p in range(PAIRS)], axis=1)
    dx_ref[...] += dot(dq, query_w[...], NT)
    dwq_ref[...] = dot(x_ref[...], dq, TN)
    put_vector(dvec_ref, N_QUERY_B, column_sum(dq.astype(f32)))


def tail_table(dkr_ref, dqr_ref, pos_ref, table_ref, vec_ref, query_w, key_w, dwq_ref, dwk_ref, dtable_ref, dvec_ref):
    JR = reversal()
    second = iotas(512, 128)[0] == 1
    tabs = {N_KEY_B: jnp.concatenate([SC * dkr_ref[p] for p in range(PAIRS)], axis=1)}
    parts = []
    for p in range(PAIRS):
        part = dqr_ref[p].T
        parts.append(SC * (part[:512] + jnp.where(second, column_sum(part[512:]), 0.0)))
    tabs[N_QUERY_B] = jnp.concatenate(parts, axis=1)
    dpos = None
    for w, dw, name in ((key_w, dwk_ref, N_KEY_B), (query_w, dwq_ref, N_QUERY_B)):
        tab = tabs[name]
        if name == N_KEY_B:
            dw[...] = dot2(pos_ref[...], tab, TN)
            put_vector(dvec_ref, name, column_sum(tab))
        else:
            dw[...] += dot2(pos_ref[...], tab, TN)
            add_vector(dvec_ref, name, column_sum(tab))
        part = dot2(tab, w[...], NT)
        dpos = part if dpos is None else dpos + part
    table = jnp.concatenate([dot(JR, table_ref[128 * b : 128 * b + 128, :]) for b in reversed(range(4))], axis=0)
    unit, inverse = normalized(pltpu.roll(table, 1, 0))
    put_vector(dvec_ref, N_REL_GAIN, column_sum(dpos * unit))
    put_vector(dvec_ref, N_REL_SHIFT, column_sum(dpos))
    dpos = pltpu.roll(norm_back(dpos, vector(vec_ref, N_REL_GAIN), unit, inverse), 511, 0).astype(bf)
    for b in range(4):
        dtable_ref[128 * b : 128 * b + 128, :] = dot(JR, dpos[128 * (3 - b) : 128 * (4 - b)])


def tail_keys(dkc_ref, dkp_ref, dv_ref, halo_ref, x_ref, key_w, value_w, dx_ref, dwk_ref, dwv_ref, dvec_ref):
    tokens = dx_ref.shape[0]
    x = x_ref[...]
    for which, (ref, w, dw, name) in enumerate(((None, key_w, dwk_ref, N_KEY_B), (dv_ref, value_w, dwv_ref, N_VALUE_B))):
        pieces = []
        for p in range(PAIRS):
            middle = slice(SPAN, SPAN + tokens)
            own = SC * (dkc_ref[p, middle, :] + dkp_ref[p, middle, :]) if ref is None else ref[p, middle, :]
            edge = [halo_ref[side, which, p].astype(f32) for side in (0, 1)]
            pieces.append(jnp.concatenate([own[:SPAN] + edge[0], own[SPAN : tokens - SPAN], own[tokens - SPAN :] + edge[1]], axis=0).astype(bf))
        d = jnp.concatenate(pieces, axis=1)
        dx_ref[...] += dot(d, w[...], NT)
        if name == N_KEY_B:
            dw[...] += dot(x, d, TN)
            add_vector(dvec_ref, name, column_sum(d.astype(f32)))
        else:
            dw[...] = dot(x, d, TN)
            put_vector(dvec_ref, name, column_sum(d.astype(f32)))


def beside(grid, step):
    return {"seq": lax.axis_index("seq") + step, "row": lax.axis_index("row")}


def seq_edges(grid):
    s = lax.axis_index("seq")
    return s > 0, s < grid.seq - 1


def enter_all(grid, p):
    sem = pltpu.get_barrier_semaphore()
    total = jnp.int32(0)
    before, after = seq_edges(grid)
    targets = [(grid.device(q), cond) for _, q, cond in neighbours_of(grid, p)]
    targets += [(beside(grid, -1), before), (beside(grid, 1), after)]
    for device, cond in targets:
        guarded(cond, lambda device=device: pl.semaphore_signal(sem, inc=1, device_id=device, device_id_type=MESH))
        total = total + (1 if cond is None else cond.astype(jnp.int32))
    pl.semaphore_wait(sem, total)


def remote(source, target, send_sem, recv_sem, device):
    return pltpu.make_async_remote_copy(
        src_ref=source, dst_ref=target, send_sem=send_sem, recv_sem=recv_sem, device_id=device, device_id_type=MESH)


def assemble(grid, shard, slots, wide, first, final):
    for k in range(grid.count):
        low, high = shard * k // GROUP, -(-shard * (k + 1) // GROUP)
        shared = k + 1 < grid.count and shard * (k + 1) % GROUP != 0
        begin = max(first, low + (1 if k > 0 and shard * k % GROUP != 0 else 0))
        end = min(final, high - (1 if shared else 0))
        block = slots.at[grid.place(k)]
        if end > begin:
            wide[16 * (begin - first) : 16 * (end - first), :] = block[16 * (begin - low) : 16 * (end - low), :].astype(f32)
        if shared and first <= high - 1 < final:
            at = high - 1
            both_parts = block[16 * (at - low) : 16 * (at - low) + 16, :].astype(f32) + slots.at[grid.place(k + 1)][0:16, :].astype(f32)
            wide[16 * (at - first) : 16 * (at - first) + 16, :] = both_parts


def unpack(wide, first, outs):
    place = matrix_rows()
    for name, out in outs.items():
        base, rows, pieces = place[name]
        for c in range(pieces):
            out[:, 128 * c : 128 * c + 128] = wide[pl.ds(base - 16 * first + c, rows, stride=pieces), :].astype(bf)


VMEM = pl.BlockSpec(memory_space=pltpu.VMEM)
ANY = pl.BlockSpec(memory_space=pl.ANY)
FEED_FROM, FEED_TO = FEED_FIRST * 128, (FEED_FIRST + FEED_ROWS) * 128
LATE = (N_OUTPUT_W, N_UP_W, N_DOWN_W)


def projected(T):
    shape = jax.ShapeDtypeStruct
    E = T + 2 * SPAN
    natural = {N_Q: (T, 128), N_Q_TURNED: (128, T), N_K: (E, 128), N_K_TURNED: (128, E), N_K_TURNED_BACK: (128, E), N_V: (E, 128), N_V_TURNED: (128, E)}
    tables = {N_KRT: (512, 128), N_KRT_TURNED: (128, 512), N_QRT: (1024, 128), N_QRT_TURNED: (128, 640)}
    out = {name: shape((PAIRS,) + extent, bf) for name, extent in (natural | tables).items()}
    out[N_KRT] = shape((2 * PAIRS, 512, 128), bf)
    out[N_POS] = shape((512, D), bf)
    out[N_CTX] = shape((PAIRS, T, 128), bf)
    out[N_E] = shape((PAIRS, T // 128, 640, 256), bf)
    out[N_INV] = shape((PAIRS, T // 128, 8, 256), f32)
    return out


def front_outputs(T):
    shape = jax.ShapeDtypeStruct
    proj = projected(T)
    place = matrix_rows()
    out = {name: proj[name] for name in (N_Q, N_K_TURNED, N_K_TURNED_BACK, N_V, N_KRT_TURNED, N_QRT, N_QRT_TURNED, N_POS, N_E, N_INV)}
    for name in (N_QUERY_W, N_KEY_W, N_VALUE_W, N_REL_TABLE):
        out[name] = shape((place[name][1], 128 * place[name][2]), bf)
    out[N_VEC] = shape((vector_rows()[1], 128), f32)
    out[N_OUT] = shape((T, D), bf)
    out[N_DZ1] = shape((T, D), f32)
    out[N_DCTX_TURNED] = shape((PAIRS, 128, T), bf)
    out[N_DFLAT] = shape((FEED_ROWS, 128), bf)
    out[N_DVEC] = shape((vector_rows()[1], 128), f32)
    return out


def front_held(T):
    shape = jax.ShapeDtypeStruct
    proj = projected(T)
    place = matrix_rows()
    held = {name: proj[name] for name in (N_Q_TURNED, N_K, N_V_TURNED, N_KRT, N_CTX)}
    for name in LATE:
        held[name] = shape((place[name][1], 128 * place[name][2]), bf)
    held[N_X_EXT] = shape((T + 2 * SPAN, D), bf)
    held[N_SEG_EXT] = shape((8, T + 2 * SPAN), jnp.int32)
    return held


def shifted_block(values, shift):
    lane = iotas(*values.shape)[1]
    moved = pltpu.roll(values, shift % 128, 1)
    moved = jnp.where(lane < shift % 128, pltpu.roll(moved, 1, 0), moved)
    return pltpu.roll(moved, shift // 128, 0)


def middle_stages(grid, p, slots, send_sem, recv_sem, groups):
    top = grid.size["z"] - 1
    z, y, c, x = p["z"], p["y"], p["c"], p["x"]
    inner = pl.ds(1, top - 1)
    half = 16 * (groups // 2)
    halves = (pl.ds(0, half), pl.ds(half, 16 * groups - half))
    middle = lambda at: jnp.logical_and(at > 0, at < top)
    flips = {axis: dict(p, **{axis: 1 - p[axis]}) for axis in ("y", "c", "x")}

    def line(at, up):
        block = slots.at[at, y, c, x]
        q = dict(p, z=z + (1 if up else -1))
        return remote(block, block, send_sem.at[1 if up else 0, at], recv_sem.at[at], grid.device(q))

    def sends(distance):
        found = [(both([middle(z - distance), z < top]), line(z - distance, True))]
        found.append((both([middle(z + distance), z > 0]), line(z + distance, False)))
        return found

    def take(distance):
        for at in (z - distance, z + distance):
            pl.when(middle(at))(lambda at=at: line(at, True).wait_recv())

    def pass_on(distance):
        for cond, copy in sends(distance):
            pl.when(cond)(copy.start)

    def across(i, first):
        axis = ("y", "x")[i] if first else ("x", "y")[i]
        part = (y, c, x) if first else ((y, c, slice(None)) if axis == "y" else (slice(None), c, x))
        block = slots.at[(inner,) + part + (halves[i], slice(None))]
        at = top + 1 + 2 * i + (0 if first else 1)
        return remote(block, block, send_sem.at[i, top + 1 + (0 if first else 1)], recv_sem.at[at], grid.device(flips[axis]))

    def hand_over():
        block = slots.at[inner, :, c]
        return remote(block, block, send_sem.at[0, top + 3], recv_sem.at[top + 5], grid.device(flips["c"]))

    def begin():
        pass_on(0)

    def second():
        take(1)
        pass_on(1)

    def third():
        for distance in range(2, top):
            take(distance)
            if distance < top - 1:
                pass_on(distance)
        for i in (0, 1):
            across(i, True).start()

    def fourth():
        for i in (0, 1):
            across(i, True).wait_recv()
        for i in (0, 1):
            across(i, False).start()

    def fifth():
        for i in (0, 1):
            across(i, False).wait_recv()
        hand_over().start()

    def finish():
        hand_over().wait_recv()
        hand_over().wait_send()
        for i in (0, 1):
            across(i, True).wait_send()
            across(i, False).wait_send()
        for distance in range(top - 1):
            for cond, copy in sends(distance):
                pl.when(cond)(copy.wait_send)

    return [begin, second, third, fourth, fifth, finish]


def front_kernel(grid, shard, slot_ref, seg_ref, x_any, og_any, *refs):
    tokens = x_any.shape[0]
    blocks = tokens // 128
    outs, held = front_outputs(tokens), front_held(tokens)
    target = dict(zip(outs, refs))
    names = list(outs) + list(held)
    here = dict(zip(names, refs[len(outs) :]))
    slots, og_ref, local_sem, out_sem, send_sem, recv_sem, late_send, late_recv, halo_send, halo_recv = refs[len(outs) + len(names) :]
    p = grid.here()
    _, groups = shard_groups(shard, grid.count)
    before, after = seq_edges(grid)
    early = lambda o: jnp.logical_or(o["z"] == 0, o["z"] == grid.size["z"] - 1)
    x_ext, seg_ext = here[N_X_EXT], here[N_SEG_EXT]
    own = pltpu.make_async_copy(x_any, x_ext.at[pl.ds(SPAN, tokens), :], local_sem.at[0])
    own.start()
    og_load = pltpu.make_async_copy(og_any, og_ref, local_sem.at[1])
    og_load.start()
    if grid.split:
        k = grid.flat(p)
        slots[p["z"], p["y"], p["c"], p["x"]] = shifted_block(slot_ref[...], k * shard % GROUP).astype(bf)
    else:
        for k in range(grid.count):
            slots[grid.place(k)] = slot_ref[k]
    seg_ext[:, SPAN : SPAN + tokens] = jnp.broadcast_to(seg_ref[...] + 1, (8, tokens))
    enter_all(grid, p)
    own.wait()

    def halo_copies(side):
        step = -1 if side == 0 else 1
        take = pl.ds(SPAN, SPAN) if side == 0 else pl.ds(tokens, SPAN)
        land = pl.ds(tokens + SPAN, SPAN) if side == 0 else pl.ds(0, SPAN)
        return [
            remote(x_ext.at[take, :], x_ext.at[land, :], halo_send.at[side, 0], halo_recv.at[side, 0], beside(grid, step)),
            remote(seg_ext.at[:, take], seg_ext.at[:, land], halo_send.at[side, 1], halo_recv.at[side, 1], beside(grid, step)),
        ]

    def start(side):
        for copy in halo_copies(side):
            copy.start()

    def sent(side):
        for copy in halo_copies(side):
            copy.wait_send()

    def landed(side):
        for copy in halo_copies(side):
            copy.wait_recv()

    first_levels, first_partners, first_ends = ([[]], [], [])
    stages = [lambda: None]
    if grid.split:
        gather = Gather(grid, p, slots, send_sem, recv_sem, groups)
        first_levels, first_partners, first_ends = gather.plan(early, False, 0)
        stages = middle_stages(grid, p, slots, late_send, late_recv, groups)
    perform(first_levels[0])
    pl.when(before)(lambda: start(0))
    pl.when(after)(lambda: start(1))

    def clear(rows):
        x_ext[rows, :] = jnp.zeros((SPAN, D), bf)
        seg_ext[:, rows] = jnp.zeros((8, SPAN), jnp.int32)

    pl.when(jnp.logical_not(before))(lambda: clear(pl.ds(0, SPAN)))
    pl.when(jnp.logical_not(after))(lambda: clear(pl.ds(tokens + SPAN, SPAN)))
    for level in first_levels[1:]:
        perform(level)
    perform(first_partners)
    perform(first_ends)
    place = matrix_rows()
    feed_group, end_group = FEED_FIRST // 16, (FEED_FIRST + FEED_ROWS) // 16
    all_groups = flat_rows(shard, grid.count) // 16

    def first_part(wide):
        assemble(grid, shard, slots, wide, 0, feed_group)
        unpack(wide, 0, {name: here[name] for name in (N_QUERY_W, N_KEY_W, N_VALUE_W)})
        assemble(grid, shard, slots, wide, end_group, all_groups)
        unpack(wide, end_group, {N_REL_TABLE: here[N_REL_TABLE]})
        vec_at, vec_total = vector_rows()
        here[N_VEC][...] = jnp.zeros((vec_total, 128), f32)
        for name in VECTORS:
            base, _, pieces = place[name]
            at = base - 16 * end_group
            here[N_VEC][vec_at[name][0] : vec_at[name][0] + pieces, :] = wide[at : at + pieces, :]

    pl.run_scoped(first_part, pltpu.VMEM((16 * max(feed_group, all_groups - end_group), 128), f32))
    pl.when(before)(lambda: sent(0))
    pl.when(after)(lambda: sent(1))
    pl.when(after)(lambda: landed(0))
    pl.when(before)(lambda: landed(1))
    stages[0]()
    project_body(x_ext, *[here[n] for n in (N_QUERY_W, N_KEY_W, N_VALUE_W, N_REL_TABLE, N_VEC, N_Q, N_Q_TURNED, N_K, N_K_TURNED, N_K_TURNED_BACK, N_V, N_V_TURNED, N_KRT, N_KRT_TURNED, N_QRT, N_QRT_TURNED, N_POS)])

    def hook(m):
        for at, stage in zip((0, 2, 4, 8), stages[1:-1]):
            pl.when(m == at)(stage)

    def attend(*scratch):
        att_fwd_body(blocks, *[here[n] for n in (N_Q_TURNED, N_K, N_V_TURNED, N_KRT, N_QRT_TURNED, N_SEG_EXT, N_CTX, N_E, N_INV)], *scratch, hook)

    pl.run_scoped(attend, pltpu.VMEM((2 * (blocks + 4), 2, 128, 640), bf), pltpu.VMEM((blocks, 640, 128), f32), *FORWARD_SCRATCH)
    leaving = {name: pltpu.make_async_copy(here[name], target[name], out_sem.at[i]) for i, name in enumerate(outs)}
    finished = (N_OUT, N_DZ1, N_DCTX_TURNED, N_DFLAT, N_DVEC)
    for name in outs:
        if name not in finished:
            leaving[name].start()
    stages[-1]()

    def second_part(wide):
        assemble(grid, shard, slots, wide, feed_group, end_group)
        unpack(wide, feed_group, {name: here[name] for name in LATE})

    pl.run_scoped(second_part, pltpu.VMEM((FEED_ROWS, 128), f32))

    og_load.wait()

    def feed_part(wide, *scratch):
        feed_body(*[x_ext, here[N_CTX], og_ref] + [here[n] for n in LATE + (N_VEC, N_OUT, N_DZ1, N_DCTX_TURNED)], wide, here[N_DVEC], *scratch)
        here[N_DFLAT][...] = wide[...].astype(bf)

    pl.run_scoped(
        feed_part, pltpu.VMEM((FEED_ROWS, 128), f32), pltpu.VMEM((tokens, D), bf), pltpu.VMEM((tokens, FF), bf), pltpu.VMEM((tokens, FF), bf),
        pltpu.VMEM((tokens, D), bf), pltpu.VMEM((tokens, D), bf), pltpu.VMEM((256, FF), f32))
    for name in finished:
        leaving[name].start()
    for name in outs:
        leaving[name].wait()


FORWARD_SCRATCH = (
    [pltpu.VMEM((640, 256), f32)] * 2 + [pltpu.VMEM((512, 256), f32)] * 2 + [pltpu.VMEM((640, 256), f32)] * 2 + [pltpu.VMEM((8, 256), f32)] * 2
)


def front(grid, shard, slot, x, seg, out_grad):
    tokens = x.shape[0]
    _, groups = shard_groups(shard, grid.count)
    outs, held = front_outputs(tokens), front_held(tokens)
    if not grid.split:
        slot = lax.all_gather(slot, ("seq", "row"))
    results = pl.pallas_call(
        functools.partial(front_kernel, grid, shard),
        out_shape=list(outs.values()),
        in_specs=[VMEM, VMEM, ANY, ANY],
        out_specs=[ANY] * len(outs),
        scratch_shapes=[pltpu.VMEM(a.shape, a.dtype) for a in list(outs.values()) + list(held.values())]
        + [
            pltpu.VMEM((grid.size["z"], grid.size["y"], 2, grid.size["x"], 16 * groups, 128), bf),
            pltpu.VMEM((tokens, D), bf),
            pltpu.SemaphoreType.DMA((2,)),
            pltpu.SemaphoreType.DMA((len(outs),)),
            pltpu.SemaphoreType.DMA((count_sends(grid, groups, False) if grid.split else 1,)),
            pltpu.SemaphoreType.DMA((2, grid.count)),
            pltpu.SemaphoreType.DMA((2, grid.size["z"] + 3)),
            pltpu.SemaphoreType.DMA((grid.size["z"] + 5,)),
            pltpu.SemaphoreType.DMA((2, 2)),
            pltpu.SemaphoreType.DMA((2, 2)),
        ],
        compiler_params=pltpu.CompilerParams(collective_id=0, has_side_effects=True, vmem_limit_bytes=62 << 20),
    )(slot, seg, x, out_grad)
    return dict(zip(outs, results))


def back_scratch(grid, shard, tokens):
    _, groups = shard_groups(shard, grid.count)
    rows = flat_rows(shard, grid.count)
    names, half, blocks = len(direction_names(grid)), (grid.count // 2 if grid.split else 1), tokens // 128
    square = pltpu.VMEM((D, D), bf)
    accumulator = pltpu.VMEM((PAIRS, tokens + 2 * SPAN, 128), f32)
    rim = pltpu.VMEM((2, 2, PAIRS, SPAN, 128), bf)
    return (
        [square, square, square, pltpu.VMEM((2 * SPAN, D), bf), pltpu.VMEM((512, D), bf), pltpu.VMEM((tokens, D), bf), pltpu.VMEM((tokens, D), f32)]
        + [pltpu.VMEM((PAIRS, tokens, 128), bf), accumulator, accumulator, accumulator, pltpu.VMEM((PAIRS, 512, 128), f32), pltpu.VMEM((PAIRS, 128, 640), f32)]
        + [pltpu.VMEM((2 * (blocks + 4), 2, 128, 640), bf), pltpu.VMEM((640, 256), f32), pltpu.VMEM((512, 256), f32)]
        + [pltpu.VMEM((640, 256), bf)] * 2 + [pltpu.VMEM((512, 256), bf)] * 2 + [pltpu.VMEM((4, 640, 256), bf), pltpu.SemaphoreType.DMA((2,))]
        + [pltpu.VMEM((D, D), f32)] * 3 + [pltpu.VMEM((2 * SPAN, D), f32), pltpu.VMEM((vector_rows()[1], 128), f32)]
        + [pltpu.VMEM((max(3 * D, rows - FEED_FIRST - FEED_ROWS), 128), f32), pltpu.VMEM((rows, 128), bf)]
        + [pltpu.VMEM((names, half, 16 * groups, 128), bf), pltpu.VMEM((16 * groups, 128), f32)]
        + [rim, rim, pltpu.SemaphoreType.DMA((8,)), pltpu.SemaphoreType.DMA((scatter_sends(grid, groups, False) + scatter_sends(grid, groups, True) if grid.split else 1,))]
        + [pltpu.SemaphoreType.DMA((2, names, half)), pltpu.SemaphoreType.DMA((2,)), pltpu.SemaphoreType.DMA((2,))]
    )


def back_kernel(grid, shard, q_ref, kT_ref, kTr_ref, v_ref, krtT_ref, qrt_ref, qrtT_ref, dctxT_ref, e_ref, inv_ref, vec_ref, dvec_in, *refs):
    sources, (dx_out, sum_ref) = refs[:8], refs[8:10]
    query_w, key_w, value_w, table_ref, pos_ref, x_ref, dx_ref = refs[10:17]
    dq, dkc, dkp, dv, dkr, dqr = refs[17:23]
    work = refs[23:32]
    dwq, dwk, dwv, dtable, dvec_ref, wide, flat, kids, total, halo_out, halo_in, load_sem, send_sem, recv_sem, halo_send, halo_recv = refs[32:]
    p = grid.here()
    tokens = dx_ref.shape[0]
    blocks = tokens // 128
    _, groups = shard_groups(shard, grid.count)
    before, after = seq_edges(grid)
    feed = pl.ds(FEED_FIRST, FEED_ROWS)
    targets = (flat.at[feed, :], query_w, key_w, value_w, table_ref, pos_ref, x_ref, dx_ref)
    loads = [pltpu.make_async_copy(source, target, load_sem.at[i]) for i, (source, target) in enumerate(zip(sources, targets))]
    for load in loads:
        load.start()
    enter_all(grid, p)
    first_row = lambda k: (k * shard // GROUP) * 16
    early = lambda k: jnp.logical_and(first_row(k) >= FEED_FIRST, first_row(k) + 16 * groups <= FEED_FIRST + FEED_ROWS)
    gifts, levels, ends, last_gifts, last_levels, last_ends = ([], [], [], [], [], [])
    if grid.split:
        scatter = lambda: Scatter(grid, p, flat, first_row, kids, total, send_sem, recv_sem, groups)
        gifts, levels, ends = scatter().plan(sum_ref, early, True, 0)
        last_gifts, last_levels, last_ends = scatter().plan(sum_ref, lambda k: jnp.logical_not(early(k)), False, scatter_sends(grid, groups, True))
    loads[0].wait()
    perform(gifts)

    def hook(m):
        for i, level in enumerate(levels):
            pl.when(m == min(2 * i + 1, PAIRS * blocks // 2 - 1))(lambda level=level: perform(level))

    att_bwd_body(blocks, q_ref, kT_ref, kTr_ref, v_ref, krtT_ref, qrt_ref, qrtT_ref, dctxT_ref, e_ref, inv_ref, dq, dkc, dkp, dv, dkr, dqr, *work, hook)
    rims = (pl.ds(0, SPAN), pl.ds(tokens + SPAN, SPAN))
    for side in (0, 1):
        halo_out[side, 0] = (SC * (dkc[:, rims[side], :] + dkp[:, rims[side], :])).astype(bf)
        halo_out[side, 1] = dv[:, rims[side], :].astype(bf)

    def halo_copy(side):
        return remote(halo_out.at[side], halo_in.at[1 - side], halo_send.at[side], halo_recv.at[1 - side], beside(grid, -1 if side == 0 else 1))

    pl.when(before)(lambda: halo_copy(0).start())
    pl.when(after)(lambda: halo_copy(1).start())

    def clear(side):
        halo_in[side] = jnp.zeros(halo_in.shape[1:], bf)

    pl.when(jnp.logical_not(before))(lambda: clear(0))
    pl.when(jnp.logical_not(after))(lambda: clear(1))
    for load in loads[1:]:
        load.wait()
    dvec_ref[...] = dvec_in[...]
    tail_local(dq, x_ref, query_w, dx_ref, dwq, dvec_ref)
    tail_table(dkr, dqr, pos_ref, table_ref, vec_ref, query_w, key_w, dwq, dwk, dtable, dvec_ref)
    pl.when(before)(lambda: halo_copy(0).wait_send())
    pl.when(after)(lambda: halo_copy(1).wait_send())
    pl.when(before)(lambda: halo_copy(1).wait_recv())
    pl.when(after)(lambda: halo_copy(0).wait_recv())
    tail_keys(dkc, dkp, dv, halo_in, x_ref, key_w, value_w, dx_ref, dwk, dwv, dvec_ref)
    leave = pltpu.make_async_copy(dx_ref, dx_out, load_sem.at[0])
    leave.start()
    place = matrix_rows()
    vec_at, _ = vector_rows()
    final = FEED_FIRST + FEED_ROWS
    for name, ref in ((N_QUERY_W, dwq), (N_KEY_W, dwk), (N_VALUE_W, dwv)):
        base, rows, pieces = place[name]
        for c in range(pieces):
            wide[pl.ds(c, rows, stride=pieces), :] = ref[:, 128 * c : 128 * c + 128]
        flat[base : base + rows * pieces, :] = wide[0 : rows * pieces, :].astype(bf)
    rest = flat.shape[0] - final
    wide[0:rest, :] = jnp.zeros((rest, 128), f32)
    base, rows, pieces = place[N_REL_TABLE]
    for c in range(pieces):
        wide[pl.ds(base - final + c, rows, stride=pieces), :] = dtable[:, 128 * c : 128 * c + 128]
    for name in VECTORS:
        base, _, pieces = place[name]
        wide[base - final : base - final + pieces, :] = dvec_ref[vec_at[name][0] : vec_at[name][0] + pieces, :]
    flat[final:, :] = wide[0:rest, :].astype(bf)
    if not grid.split:
        sum_ref[...] = flat[...]
    perform(last_gifts)
    for level in last_levels:
        perform(level)
    perform(ends)
    perform(last_ends)
    leave.wait()


def back(grid, shard, f, x):
    _, groups = shard_groups(shard, grid.count)
    tokens = x.shape[0]
    shape = jax.ShapeDtypeStruct
    leaving = shape((16 * groups, 128), f32) if grid.split else shape((flat_rows(shard, grid.count), 128), bf)
    dx, summed = pl.pallas_call(
        functools.partial(back_kernel, grid, shard),
        out_shape=[shape((tokens, D), f32), leaving],
        in_specs=[VMEM] * 8 + [ANY] + [VMEM] * 3 + [ANY] * 8,
        out_specs=[ANY, VMEM],
        scratch_shapes=back_scratch(grid, shard, tokens),
        compiler_params=pltpu.CompilerParams(collective_id=1, has_side_effects=True, vmem_limit_bytes=62 << 20),
    )(
        *[f[n] for n in (N_Q, N_K_TURNED, N_K_TURNED_BACK, N_V, N_KRT_TURNED, N_QRT, N_QRT_TURNED, N_DCTX_TURNED, N_E, N_INV, N_VEC, N_DVEC)],
        *[f[n] for n in (N_DFLAT, N_QUERY_W, N_KEY_W, N_VALUE_W, N_REL_TABLE, N_POS)], x, f[N_DZ1])
    if not grid.split:
        first, _ = shard_groups(shard, grid.count)
        pieces = jnp.concatenate([summed[16 * at : 16 * (at + groups)] for at in first], axis=0)
        summed = lax.psum_scatter(pieces.astype(f32), ("seq", "row"), scatter_dimension=0, tiled=True)
    return dx, summed


def on_device(layer_input, segment_ids, out_grad, weights, momentum, average):
    tokens_here = layer_input.shape[1]
    grid = Grid(lax.axis_size("seq"), lax.axis_size("row"))
    shard = weights.shape[0]
    _, groups = shard_groups(shard, grid.count)
    shift = (lax.axis_index("seq") * grid.row + lax.axis_index("row")) * shard % GROUP
    slot = jnp.pad(weights, (0, GROUP * groups - shard)).reshape(16 * groups, 128)
    if not grid.split:
        slot = lax.dynamic_update_slice(jnp.zeros((GROUP * groups,), bf), weights.astype(bf), (shift,)).reshape(16 * groups, 128)
    f = front(grid, shard, slot, layer_input[0], segment_ids, out_grad[0])
    block_output = f[N_OUT]
    dx, summed = back(grid, shard, f, layer_input[0])
    weight_grad = lax.dynamic_slice(summed.reshape(-1), (shift,), (shard,))
    all_tokens = tokens_here * grid.seq * layer_input.shape[0] * grid.row
    rate = 0.1 / math.sqrt(all_tokens)
    new_momentum = 0.5 * momentum + weight_grad
    new_weights = weights - rate * (weight_grad + 0.5 * new_momentum)
    new_average = 0.5 * average + 0.5 * new_weights
    return (
        block_output[None],
        dx[None],
        weight_grad,
        new_momentum,
        new_average,
        new_weights,
        new_weights.astype(jnp.bfloat16),
    )


def solution(mesh):
    flat = P(("seq", "row"))
    tokens = P("row", "seq", None)
    return jax.shard_map(
        on_device,
        mesh=mesh,
        in_specs=(tokens, P("row", "seq"), tokens, flat, flat, flat),
        out_specs=(tokens, tokens, flat, flat, flat, flat, flat),
        check_vma=False,
    )
```

profile of v0, /device:TPU:0, one launch (start us, length us, event | category | flops | bytes accessed | tf_op | source)
XLA Modules:
  0.0 172.3 jit_solution(3459577610618565569)
XLA Ops:
  0.6 1.7 pad_bitcast_fusion.slot_ref
  2.3 82.8 %shard_map.117 = (bf16[3,1024,128]{2,1,0:T(8,128)(2,1)}, bf16[3,128,1536]{2,1,0:T(8,128)(2,1)}, bf16[3,128,1536]{2,1,0:T(8,128)(2,1)}, bf16[3,1536,128]{2,1,0:T(...) custom-call(f32[512,128]{1,0:T(8,128)} %pad_bitcast_fusion.slot_ref,, ...), custom_call_target="tpu_custom_call" | custom-call | tf_op jit(solution)/shard_map/pallas_call | solution.py:1244
  85.1 0.0 copy-start.2
  85.1 0.0 copy-start.4
  85.2 82.2 %shard_map.118 = (f32[1024,384]{1,0:T(8,128)}, f32[512,128]{1,0:T(8,128)}) custom-call(bf16[3,1024,128]{2,1,0:T(8,128)(2,1)} %get-tuple-element.30.q_ref, bf16[3,128,1536]{2,1,0:T(8,128)(2,1)} %get-tuple-element.31.kT_ref, bf16[3,128,1536]{2,1,0:T(8,128)(2,1)} %get-tuple-element.32.kTr_ref, bf16[3,1536,128]{2,1,0:T(8,128)(2,1)} %get-tuple-element.33.v_ref, ...), custom_call_target="tpu_custom_call" | custom-call | tf_op jit(solution)/shard_map/pallas_call | solution.py:1379
  167.3 0.0 copy-start.5
  167.4 0.0 copy-start.3
  167.4 0.0 copy-done.2
  167.4 0.0 copy-done.4
  167.4 0.0 copy-start
  167.4 2.1 %fusion = (bf16[61620]{0:T(1024)(128)(2,1)}, f32[61620]{0:T(1024)S(1)}, f32[61620]{0:T(1024)}, f32[61620]{0:T(1024)}) fusion(f32[61620]{0:T(1024)S(1)} %copy-done.2, f32[61620]{0:T(1024)S(1)} %copy-done.4, f32[65536]{0:T(1024)} %bitcast.12, s32[]{:T(128)S(6)} %select_n.11), kind=kLoop, calls=%fused_computation.4 | loop fusion | flops 431340 | bytes 1602124 | tf_op jit(solution)/shard_map/convert_element_type | solution.py:1421
  169.5 0.0 copy-start.1
  169.5 0.0 copy-done.5
  169.5 0.8 add_multiply_fusion
  170.3 0.0 copy-done.3
  170.3 0.9 copy.15
  171.2 0.0 copy-done
  171.2 1.1 copy.16
  172.3 0.0 copy-done.1
Async XLA Ops:
  85.1 82.3 %copy-start.2 = (f32[61620]{0:T(1024)S(1)}, f32[61620]{0:T(1024)}, u32[]{:S(2)}) copy-start(f32[61620]{0:T(1024)} %param.9) | copy-start | bytes 739444
  85.1 82.3 %copy-start.4 = (f32[61620]{0:T(1024)S(1)}, f32[61620]{0:T(1024)}, u32[]{:S(2)}) copy-start(f32[61620]{0:T(1024)} %param.10) | copy-start | bytes 739444
  167.3 2.1 %copy-start.5 = (f32[61620]{0:T(1024)S(1)}, f32[61620]{0:T(1024)}, u32[]{:S(2)}) copy-start(f32[61620]{0:T(1024)} %param.11) | copy-start | bytes 739444
  167.4 2.9 %copy-start.3 = (bf16[1024,384]{1,0:T(8,128)(2,1)S(1)}, bf16[1024,384]{1,0:T(8,128)(2,1)}, u32[]{:S(2)}) copy-start(bf16[1024,384]{1,0:T(8,128)(2,1)} %get-tuple-element.29) | copy-start | bytes 2359300
  167.4 3.8 %copy-start = (f32[1024,384]{1,0:T(8,128)S(1)}, f32[1024,384]{1,0:T(8,128)}, u32[]{:S(2)}) copy-start(f32[1024,384]{1,0:T(8,128)} %get-tuple-element.49) | copy-start | bytes 4718596
  169.5 2.8 %copy-start.1 = (f32[61620]{0:T(1024)}, f32[61620]{0:T(1024)S(1)}, u32[]{:S(2)}) copy-start(f32[61620]{0:T(1024)S(1)} %get-tuple-element.67) | copy-start | bytes 739444
where the time goes:
time: 173 us; the launch traced here: 172 us
  Pallas kernels  165 us (95%)
  local copies, waits for them, and re-layouts  3.72 us (2%)
  other arithmetic  2.85 us (2%)
    pallas_call x1, Pallas kernels, front(): pl.pallas_call(functools.partial(front_kernel, grid, shard), out_shape=li...  82.8 us
    pallas_call x1, Pallas kernels, back(): pl.pallas_call(functools.partial(back_kernel, grid, shard), out_shape=[sh...  82.2 us

commit v1 on v0

--- a/solution.py
+++ b/solution.py
@@ -95,18 +95,6 @@
             o[axis] = p[axis] + d
             conds.append(p[axis] + d >= 0 if d < 0 else p[axis] + d < grid.size[axis])
     return o, both(conds)
-
-
-def parent_of(grid, p, order, off):
-    last = max((i for i, d in enumerate(off) if d != 0), default=None)
-    if last is None:
-        return None, None
-    q, axis, d = dict(p), order[last], off[last]
-    if d == "f":
-        q[axis] = 1 - p[axis]
-        return q, axis + "0"
-    q[axis] = p[axis] + (1 if d > 0 else -1)
-    return q, axis + ("+" if d > 0 else "-")
 
 
 def children_of(grid, p, order, off):
@@ -220,57 +208,43 @@
     return sum(len(children_of(grid, fake, order, off)) + 1 for order, _, _ in parts_of(groups, whole) for off in grid.offsets(order))
 
 
-OPPOSITE = {"+": "-", "-": "+", "0": "0"}
-
-
-def direction_names(grid):
-    names = ["c0"]
-    for axis in ("z", "y", "x"):
-        if grid.size[axis] == 2:
-            names.append(axis + "0")
-        elif grid.size[axis] > 2:
-            names += [axis + "+", axis + "-"]
-    return names
-
-
 class Scatter:
     def __init__(self, grid, p, flat, first_row, kids, total, send_sem, recv_sem, groups):
         self.grid, self.p, self.flat, self.first_row = grid, p, flat, first_row
         self.kids, self.total = kids, total
         self.send_sem, self.recv_sem, self.groups = send_sem, recv_sem, groups
-        self.names = direction_names(grid)
-
-    def incoming(self, part, name, place):
+
+    def incoming(self, part, kid, place):
         start, rows = self.spans[part]
-        return self.kids.at[self.names.index(name), place, pl.ds(start, rows), :]
-
-    def transfer(self, source, part, name, place, q, send):
+        return self.kids.at[kid, place, pl.ds(start, rows), :]
+
+    def transfer(self, source, part, kid, place, q, send):
         return pltpu.make_async_remote_copy(
-            src_ref=source, dst_ref=self.incoming(part, name, place), send_sem=self.send_sem.at[send],
-            recv_sem=self.recv_sem.at[part, self.names.index(name), place], device_id=self.grid.device(q), device_id_type=MESH)
-
-    def arrived(self, part, name, place):
-        block = self.incoming(part, name, place)
+            src_ref=source, dst_ref=self.incoming(part, kid, place), send_sem=self.send_sem.at[send],
+            recv_sem=self.recv_sem.at[part, kid, place], device_id=self.grid.device(q), device_id_type=MESH)
+
+    def arrived(self, part, kid, place):
+        block = self.incoming(part, kid, place)
         pltpu.make_async_remote_copy(
-            src_ref=block, dst_ref=block, send_sem=self.send_sem.at[0],
-            recv_sem=self.recv_sem.at[part, self.names.index(name), place],
+            src_ref=block, dst_ref=block, send_sem=self.send_sem.at[0], recv_sem=self.recv_sem.at[part, kid, place],
             device_id=self.grid.device(self.p), device_id_type=MESH).wait_recv()
 
     def plan(self, result, chosen, whole, used):
         grid, p = self.grid, self.p
         sibling = dict(p)
         sibling["c"] = 1 - p["c"]
+        along = {"y": 1, "x": 2}
         gifts, levels, ends = [], {}, []
         self.spans = [part[1:] for part in parts_of(self.groups, whole)]
         for part, (order, start, rows) in enumerate(parts_of(self.groups, whole)):
-            for off in sorted(grid.offsets(order), key=lambda off: -sum(1 if o == "f" else abs(o) for o in off)):
-                hops = sum(1 if o == "f" else abs(o) for o in off)
+            for off in sorted(grid.offsets(order), key=lambda off: -sum(o != 0 for o in off)):
+                hops = sum(o != 0 for o in off)
                 o, cond = source_of(grid, sibling, order, off)
                 cond = both([cond, chosen(grid.flat(o))])
 
                 def give(part=part, o=o, index=used, start=start, rows=rows):
                     block = self.flat.at[pl.ds(pl.multiple_of(self.first_row(grid.flat(o)) + start, 16), rows), :]
-                    return self.transfer(block, part, "c0", grid.plane(o), sibling, index)
+                    return self.transfer(block, part, 0, grid.plane(o), sibling, index)
 
                 gifts.append((cond, lambda give=give: give().start()))
                 ends.append((cond, lambda give=give: give().wait_send()))
@@ -278,21 +252,31 @@
                 o, cond = source_of(grid, p, order, off)
                 place, k = grid.plane(o), grid.flat(o)
                 cond = both([cond, chosen(k)])
-                kids = children_of(grid, p, order, off)
-                parent, side = parent_of(grid, p, order, off)
-
-                def push(part=part, place=place, parent=parent, side=side, index=used, start=start, rows=rows):
-                    return self.transfer(self.incoming(part, "c0", place), part, side[0] + OPPOSITE[side[1]], place, parent, index)
+                last = max((i for i, d in enumerate(off) if d != 0), default=None)
+                kids = []
+                for axis in order[0 if last is None else last + 1 :]:
+                    if axis == "z":
+                        kids += [(3 + s, p["z"] != s) for s in range(grid.size["z"])]
+                    else:
+                        kids.append((along[axis], None))
+                parent, kid = None, None
+                if last is not None:
+                    parent = dict(p)
+                    parent[order[last]] = o[order[last]]
+                    kid = 3 + p["z"] if order[last] == "z" else along[order[last]]
+
+                def push(part=part, place=place, parent=parent, kid=kid, index=used):
+                    return self.transfer(self.incoming(part, 0, place), part, kid, place, parent, index)
 
                 def step(part=part, place=place, k=k, kids=kids, parent=parent, start=start, rows=rows, push=push):
-                    self.arrived(part, "c0", place)
+                    self.arrived(part, 0, place)
                     mine = self.flat[pl.ds(pl.multiple_of(self.first_row(k) + start, 16), rows), :].astype(f32)
-                    self.total[0:rows, :] = mine + self.incoming(part, "c0", place)[...].astype(f32)
-                    for name, q, when in kids:
-
-                        def add(name=name):
-                            self.arrived(part, name, place)
-                            self.total[0:rows, :] += self.incoming(part, name, place)[...].astype(f32)
+                    self.total[0:rows, :] = mine + self.incoming(part, 0, place)[...].astype(f32)
+                    for kid, when in kids:
+
+                        def add(kid=kid):
+                            self.arrived(part, kid, place)
+                            self.total[0:rows, :] += self.incoming(part, kid, place)[...].astype(f32)
 
                         guarded(when, add)
                     if parent is None:
@@ -306,6 +290,82 @@
                     ends.append((cond, lambda push=push: push().wait_send()))
                     used += 1
         return gifts, [levels[h] for h in sorted(levels)], ends
+
+
+    def plan_outer(self, result, chosen, used):
+        grid, p = self.grid, self.p
+        sibling = dict(p, c=1 - p["c"])
+        self.spans = [part[1:] for part in parts_of(self.groups, False)]
+        gifts, steps, ends = [], [], []
+        for distance in (2, 1, 0):
+            for part, (start, rows) in enumerate(self.spans):
+                for plane in (0, grid.size["z"] - 1):
+                    for fy, fx in ((1, 1), (1, 0), (0, 1), (0, 0)):
+                        if fy + fx != distance:
+                            continue
+                        o = dict(p, z=plane, y=1 - p["y"] if fy else p["y"], x=1 - p["x"] if fx else p["x"])
+                        other = dict(o, c=sibling["c"])
+                        here = p["z"] == plane
+
+                        def give(part=part, o=other, index=used, start=start, rows=rows):
+                            block = self.flat.at[pl.ds(pl.multiple_of(self.first_row(grid.flat(o)) + start, 16), rows), :]
+                            return self.transfer(block, part, 0, grid.plane(o), sibling, index)
+
+                        wanted = chosen(grid.flat(other)) if plane else None
+                        first = (0 if fx else 1 + (not fy)) if part == 0 else 1 - fy
+                        gifts.append((first, wanted, lambda give=give: give().start()))
+                        ends.append((wanted, lambda give=give: give().wait_send()))
+                        cond = chosen(grid.flat(o)) if plane else None
+                        flip_x, flip_y, straight = (dict(p, x=1 - p["x"]), 2), (dict(p, y=1 - p["y"]), 1), (dict(p, z=plane), 3 + p["z"])
+                        planes = [(3 + s, both([here, p["z"] != s])) for s in range(grid.size["z"])]
+                        if part == 0:
+                            kids = [] if fx else [(2, None)] if fy else [(2, None), (1, None)] + planes
+                            routes = [(None, flip_x)] if fx else [(None, flip_y)] if fy else [(jnp.logical_not(here), straight)]
+                        else:
+                            kids = [] if fy else [(1, None)] + planes + ([] if fx else [(2, here)])
+                            routes = [(None, flip_y)] if fy else [(jnp.logical_not(here), straight)] + ([(here, flip_x)] if fx else [])
+                        place = grid.plane(o)
+                        pushes = []
+                        for n, (when, (q, kid)) in enumerate(routes):
+
+                            def push(part=part, place=place, q=q, kid=kid, index=used + 1 + n):
+                                return self.transfer(self.incoming(part, 0, place), part, kid, place, q, index)
+
+                            pushes.append((when, push))
+                            ends.append((both([cond, when]), lambda push=push: push().wait_send()))
+                        used += 3
+
+                        def step(part=part, place=place, o=o, kids=kids, pushes=pushes, start=start, rows=rows, owner=here if fy + fx == 0 else None):
+                            self.arrived(part, 0, place)
+                            mine = self.flat[pl.ds(pl.multiple_of(self.first_row(grid.flat(o)) + start, 16), rows), :].astype(f32)
+                            self.total[0:rows, :] = mine + self.incoming(part, 0, place)[...].astype(f32)
+                            for kid, when in kids:
+
+                                def add(kid=kid):
+                                    self.arrived(part, kid, place)
+                                    self.total[0:rows, :] += self.incoming(part, kid, place)[...].astype(f32)
+
+                                guarded(when, add)
+                            self.kids[0, place, pl.ds(start, rows), :] = self.total[0:rows, :].astype(bf)
+                            for when, push in pushes:
+                                guarded(when, lambda push=push: push().start())
+                            if owner is not None:
+
+                                def finish():
+                                    result[pl.ds(start, rows), :] = self.total[0:rows, :]
+
+                                pl.when(owner)(finish)
+
+                        away = jnp.logical_not(here)
+                        if part == 0:
+                            found = [(0, None)] if fx else [(1, None)] if fy else [(2, away), (3, here)]
+                        else:
+                            found = [(0, None)] if fy else [(1, away), (2, here)] if fx else [(1, away), (3, here)]
+                        for ready, when in found:
+                            steps.append((ready, both([cond, when]), step))
+        steps.sort(key=lambda item: item[0])
+        gifts.sort(key=lambda item: item[0])
+        return [item[1:] for item in gifts], [item[1:] for item in steps], ends
 
 
 def scatter_sends(grid, groups, whole):
@@ -930,11 +990,14 @@
     return s > 0, s < grid.seq - 1
 
 
-def enter_all(grid, p):
+def enter_all(grid, p, straight=False):
     sem = pltpu.get_barrier_semaphore()
     total = jnp.int32(0)
     before, after = seq_edges(grid)
     targets = [(grid.device(q), cond) for _, q, cond in neighbours_of(grid, p)]
+    if straight:
+        for d in range(2, grid.size["z"]):
+            targets += [(grid.device(dict(p, z=p["z"] - d)), p["z"] - d >= 0), (grid.device(dict(p, z=p["z"] + d)), p["z"] + d < grid.size["z"])]
     targets += [(beside(grid, -1), before), (beside(grid, 1), after)]
     for device, cond in targets:
         guarded(cond, lambda device=device: pl.semaphore_signal(sem, inc=1, device_id=device, device_id_type=MESH))
@@ -1267,7 +1330,7 @@
 def back_scratch(grid, shard, tokens):
     _, groups = shard_groups(shard, grid.count)
     rows = flat_rows(shard, grid.count)
-    names, half, blocks = len(direction_names(grid)), (grid.count // 2 if grid.split else 1), tokens // 128
+    names, half, blocks = 3 + grid.size["z"], (grid.count // 2 if grid.split else 1), tokens // 128
     square = pltpu.VMEM((D, D), bf)
     accumulator = pltpu.VMEM((PAIRS, tokens + 2 * SPAN, 128), f32)
     rim = pltpu.VMEM((2, 2, PAIRS, SPAN, 128), bf)
@@ -1279,7 +1342,7 @@
         + [pltpu.VMEM((D, D), f32)] * 3 + [pltpu.VMEM((2 * SPAN, D), f32), pltpu.VMEM((vector_rows()[1], 128), f32)]
         + [pltpu.VMEM((max(3 * D, rows - FEED_FIRST - FEED_ROWS), 128), f32), pltpu.VMEM((rows, 128), bf)]
         + [pltpu.VMEM((names, half, 16 * groups, 128), bf), pltpu.VMEM((16 * groups, 128), f32)]
-        + [rim, rim, pltpu.SemaphoreType.DMA((8,)), pltpu.SemaphoreType.DMA((scatter_sends(grid, groups, False) + scatter_sends(grid, groups, True) if grid.split else 1,))]
+        + [rim, rim, pltpu.SemaphoreType.DMA((8,)), pltpu.SemaphoreType.DMA((scatter_sends(grid, groups, True) + 48 if grid.split else 1,))]
         + [pltpu.SemaphoreType.DMA((2, names, half)), pltpu.SemaphoreType.DMA((2,)), pltpu.SemaphoreType.DMA((2,))]
     )
 
@@ -1300,20 +1363,20 @@
     loads = [pltpu.make_async_copy(source, target, load_sem.at[i]) for i, (source, target) in enumerate(zip(sources, targets))]
     for load in loads:
         load.start()
-    enter_all(grid, p)
+    enter_all(grid, p, True)
     first_row = lambda k: (k * shard // GROUP) * 16
     early = lambda k: jnp.logical_and(first_row(k) >= FEED_FIRST, first_row(k) + 16 * groups <= FEED_FIRST + FEED_ROWS)
-    gifts, levels, ends, last_gifts, last_levels, last_ends = ([], [], [], [], [], [])
+    gifts, levels, ends, last_gifts, last_steps, last_ends = ([], [], [], [], [], [])
     if grid.split:
         scatter = lambda: Scatter(grid, p, flat, first_row, kids, total, send_sem, recv_sem, groups)
         gifts, levels, ends = scatter().plan(sum_ref, early, True, 0)
-        last_gifts, last_levels, last_ends = scatter().plan(sum_ref, lambda k: jnp.logical_not(early(k)), False, scatter_sends(grid, groups, True))
+        last_gifts, last_steps, last_ends = scatter().plan_outer(sum_ref, lambda k: jnp.logical_not(early(k)), scatter_sends(grid, groups, True))
     loads[0].wait()
     perform(gifts)
 
     def hook(m):
         for i, level in enumerate(levels):
-            pl.when(m == min(2 * i + 1, PAIRS * blocks // 2 - 1))(lambda level=level: perform(level))
+            pl.when(m == min(3 * i + 1, PAIRS * blocks // 2 - 1))(lambda level=level: perform(level))
 
     att_bwd_body(blocks, q_ref, kT_ref, kTr_ref, v_ref, krtT_ref, qrt_ref, qrtT_ref, dctxT_ref, e_ref, inv_ref, dq, dkc, dkp, dv, dkr, dqr, *work, hook)
     rims = (pl.ds(0, SPAN), pl.ds(tokens + SPAN, SPAN))
@@ -1364,8 +1427,7 @@
     if not grid.split:
         sum_ref[...] = flat[...]
     perform(last_gifts)
-    for level in last_levels:
-        perform(level)
+    perform(last_steps)
     perform(ends)
     perform(last_ends)
     leave.wait()

time: 173 us -> 171 us (0.988)
  no operation moved by 1% of the time
where the time goes in v1:
time: 171 us
  Pallas kernels  164 us (96%)
  local copies, waits for them, and re-layouts  3.72 us (2%)
  other arithmetic  2.85 us (2%)
    pallas_call x1, Pallas kernels, front(): pl.pallas_call(functools.partial(front_kernel, grid, shard), out_shape=li...  82.8 us
    pallas_call x1, Pallas kernels, back(): pl.pallas_call(functools.partial(back_kernel, grid, shard), out_shape=[sh...  80.9 us

profile of v1, /device:TPU:0, one launch (start us, length us, event | category | flops | bytes accessed | tf_op | source)
XLA Modules:
  0.0 171.1 jit_solution(906094193319875783)
XLA Ops:
  0.6 1.7 pad_bitcast_fusion.slot_ref
  2.3 82.8 %shard_map.117 = (bf16[3,1024,128]{2,1,0:T(8,128)(2,1)}, bf16[3,128,1536]{2,1,0:T(8,128)(2,1)}, bf16[3,128,1536]{2,1,0:T(8,128)(2,1)}, bf16[3,1536,128]{2,1,0:T(...) custom-call(f32[512,128]{1,0:T(8,128)} %pad_bitcast_fusion.slot_ref,, ...), custom_call_target="tpu_custom_call" | custom-call | tf_op jit(solution)/shard_map/pallas_call | solution.py:1307
  85.1 0.0 copy-start.2
  85.1 0.0 copy-start.4
  85.2 80.9 %shard_map.118 = (f32[1024,384]{1,0:T(8,128)}, f32[512,128]{1,0:T(8,128)}) custom-call(bf16[3,1024,128]{2,1,0:T(8,128)(2,1)} %get-tuple-element.30.q_ref, bf16[3,128,1536]{2,1,0:T(8,128)(2,1)} %get-tuple-element.31.kT_ref, bf16[3,128,1536]{2,1,0:T(8,128)(2,1)} %get-tuple-element.32.kTr_ref, bf16[3,1536,128]{2,1,0:T(8,128)(2,1)} %get-tuple-element.33.v_ref, ...), custom_call_target="tpu_custom_call" | custom-call | tf_op jit(solution)/shard_map/pallas_call | solution.py:1441
  166.1 0.0 copy-start.5
  166.1 0.0 copy-start.3
  166.1 0.0 copy-done.2
  166.2 0.0 copy-done.4
  166.2 0.0 copy-start
  166.2 2.1 %fusion = (bf16[61620]{0:T(1024)(128)(2,1)}, f32[61620]{0:T(1024)S(1)}, f32[61620]{0:T(1024)}, f32[61620]{0:T(1024)}) fusion(f32[61620]{0:T(1024)S(1)} %copy-done.2, f32[61620]{0:T(1024)S(1)} %copy-done.4, f32[65536]{0:T(1024)} %bitcast.12, s32[]{:T(128)S(6)} %select_n.11), kind=kLoop, calls=%fused_computation.4 | loop fusion | flops 431340 | bytes 1602124 | tf_op jit(solution)/shard_map/convert_element_type | solution.py:1483
  168.2 0.0 copy-start.1
  168.2 0.0 copy-done.5
  168.2 0.8 add_multiply_fusion
  169.0 0.0 copy-done.3
  169.0 0.9 copy.15
  169.9 0.0 copy-done
  169.9 1.1 copy.16
  171.1 0.0 copy-done.1
Async XLA Ops:
  85.1 81.0 %copy-start.2 = (f32[61620]{0:T(1024)S(1)}, f32[61620]{0:T(1024)}, u32[]{:S(2)}) copy-start(f32[61620]{0:T(1024)} %param.9) | copy-start | bytes 739444
  85.1 81.0 %copy-start.4 = (f32[61620]{0:T(1024)S(1)}, f32[61620]{0:T(1024)}, u32[]{:S(2)}) copy-start(f32[61620]{0:T(1024)} %param.10) | copy-start | bytes 739444
  166.1 2.1 %copy-start.5 = (f32[61620]{0:T(1024)S(1)}, f32[61620]{0:T(1024)}, u32[]{:S(2)}) copy-start(f32[61620]{0:T(1024)} %param.11) | copy-start | bytes 739444
  166.1 2.9 %copy-start.3 = (bf16[1024,384]{1,0:T(8,128)(2,1)S(1)}, bf16[1024,384]{1,0:T(8,128)(2,1)}, u32[]{:S(2)}) copy-start(bf16[1024,384]{1,0:T(8,128)(2,1)} %get-tuple-element.29) | copy-start | bytes 2359300
  166.2 3.8 %copy-start = (f32[1024,384]{1,0:T(8,128)S(1)}, f32[1024,384]{1,0:T(8,128)}, u32[]{:S(2)}) copy-start(f32[1024,384]{1,0:T(8,128)} %get-tuple-element.49) | copy-start | bytes 4718596
  168.2 2.8 %copy-start.1 = (f32[61620]{0:T(1024)}, f32[61620]{0:T(1024)S(1)}, u32[]{:S(2)}) copy-start(f32[61620]{0:T(1024)S(1)} %get-tuple-element.67) | copy-start | bytes 739444
